TPU v7x, 32 devices: a whole 2x2x4 slice. The times are simulated.
32 devices in a mesh: groups: 2 (over y), tok: 4 (over z), dp: 2 (over x), head: 2 (over core).
Axes of the slice: x: 2, y: 2, z: 4, core: 2. Of those that a mesh axis runs over, the one named last changes fastest.
Arguments:
- features: bfloat16 [128, 4096], P(('groups', 'dp', 'head'), 'tok'), parts along dimension 0, may hold values from -6 to 6
- cross_down: bfloat16 [4096, 512], P('tok'), may hold values from -0.09375 to 0.09375
- cross_up: bfloat16 [512, 4096], P(None, 'tok'), may hold values from -0.25 to 0.25
- cross_bias: float32 [4096], P('tok'), may hold values from -4 to 4
- feature_token: int32 [4096], P('tok'), may hold values from 0 to 31, as said below
- proj_weight: bfloat16 [32, 128, 1536], P('tok'), may hold values from -0.5 to 0.5
- proj_bias: float32 [32, 1536], P('tok'), may hold values from -3 to 3
- mix_gain: float32 [32, 1536], P('tok'), may hold values from 0.1 to 1.9
- expand_weight: bfloat16 [32, 1536, 3072], P('tok', None, ('dp', 'head')), may hold values from -0.15625 to 0.15625
- expand_bias: float32 [32, 3072], P('tok', ('dp', 'head')), may hold values from -3 to 3
- contract_weight: bfloat16 [32, 3072, 1536], P('tok', ('dp', 'head')), may hold values from -0.109375 to 0.109375
- contract_bias: float32 [32, 1536], P('tok'), may hold values from -3 to 3
- block_gain: float32 [32, 1536], P('tok'), may hold values from 0.1 to 1.9
- gate_weight: bfloat16 [1536, 1536], P(None, ('dp', 'head')), may hold values from -0.15625 to 0.15625
- gate_bias: float32 [1536], replicated, may hold values from -4 to 4
Outputs:
- gated_states: bfloat16 [8, 16, 32, 1536], P(('groups', 'dp', 'head'), 'tok'), parts along dimension 0
There are 2 independent parts, one for each index of `groups`. A program takes and returns all parts, laid end to end along the dimension named above; an argument that names none is the same for every part. Nothing has to cross between parts.
Inputs may be any that keep to these rules, and one draw needn't show every extreme that they name: `feature_token`: in every block of 128 consecutive features, each token number appears exactly 4 times.
All inputs are finite; a program needn't handle non-finite values.
Results may differ from a plain program's by a relative error of at most 0.018.
Values may be sent and summed in bfloat16 or wider, within the bound.
A program may use at most 128 MiB of HBM per device.

v0:
```python
import jax
import jax.numpy as jnp
from jax import lax
from jax.sharding import PartitionSpec as P

FEAT_TOKENS = 32
DIM = 1536


def rms_norm(values, gain_row):
    scale = lax.rsqrt(jnp.mean(values * values, axis=-1, keepdims=True) + 1e-06)
    return values * scale * gain_row


def per_device(
    features,
    cross_down,
    cross_up,
    cross_bias,
    feature_token,
    proj_weight,
    proj_bias,
    mix_gain,
    expand_weight,
    expand_bias,
    contract_weight,
    contract_bias,
    block_gain,
    gate_weight,
    gate_bias,
):
    rows_local = features.shape[0]
    local_tokens = proj_weight.shape[0]
    head_size = DIM // FEAT_TOKENS
    sources = lax.axis_size("tok")
    partial_low = jnp.dot(features, cross_down, preferred_element_type=jnp.float32)
    low_rank = lax.psum(partial_low.astype(jnp.bfloat16), "tok")
    lifted = jnp.dot(low_rank, cross_up, preferred_element_type=jnp.float32)
    widened = features.astype(jnp.float32)
    crossed = (widened * (lifted + cross_bias) + widened).astype(jnp.bfloat16)
    ordering = jnp.argsort(feature_token, stable=True)
    grouped = jnp.take(crossed, ordering, axis=1)
    routed = lax.all_to_all(grouped, "tok", split_axis=1, concat_axis=1, tiled=True)
    picked = (
        routed.reshape(rows_local, sources, local_tokens, -1)
        .transpose(0, 2, 1, 3)
        .reshape(rows_local, local_tokens, -1)
    )
    embedded = (
        jnp.einsum("rjf,jfd->rjd", picked, proj_weight, preferred_element_type=jnp.float32)
        + proj_bias
    )
    embedded = embedded.astype(jnp.bfloat16)
    heads_in = lax.all_to_all(embedded, "tok", split_axis=2, concat_axis=1, tiled=True)
    mixed_heads = (
        heads_in.reshape(rows_local, FEAT_TOKENS, local_tokens, head_size)
        .transpose(0, 2, 1, 3)
        .reshape(rows_local, local_tokens, DIM)
    )
    first_norm = rms_norm(
        mixed_heads.astype(jnp.float32) + embedded.astype(jnp.float32), mix_gain
    ).astype(jnp.bfloat16)
    every_row = lax.all_gather(first_norm, ("dp", "head"), axis=0, tiled=True)
    gelu_in = (
        jnp.einsum("rjd,jdh->rjh", every_row, expand_weight, preferred_element_type=jnp.float32)
        + expand_bias
    )
    activated = jax.nn.gelu(gelu_in).astype(jnp.bfloat16)
    summed = lax.psum_scatter(
        jnp.einsum(
            "rjh,jhd->rjd", activated, contract_weight, preferred_element_type=jnp.float32
        ).astype(jnp.bfloat16),
        ("dp", "head"),
        scatter_dimension=0,
        tiled=True,
    ).astype(jnp.float32)
    second_norm = rms_norm(
        summed + contract_bias + first_norm.astype(jnp.float32), block_gain
    ).astype(jnp.bfloat16)
    owned_rows = lax.all_to_all(second_norm, "tok", split_axis=0, concat_axis=1, tiled=True)
    flattened = owned_rows.reshape(-1, DIM)
    weight_piece = lax.all_gather(gate_weight, ("dp", "head"), axis=1, tiled=True)
    col_count = weight_piece.shape[1]
    logits = jnp.dot(flattened, weight_piece, preferred_element_type=jnp.float32).reshape(
        owned_rows.shape[0], owned_rows.shape[1], col_count
    )
    kept_cols = owned_rows.astype(jnp.float32)
    result = (kept_cols * jax.nn.sigmoid(logits + gate_bias)).astype(jnp.bfloat16)
    return result[None]


def solution(mesh):
    placed = (
        P(("groups", "dp", "head"), "tok"),
        P("tok", None),
        P(None, "tok"),
        P("tok"),
        P("tok"),
        P("tok", None, None),
        P("tok", None),
        P("tok", None),
        P("tok", None, ("dp", "head")),
        P("tok", ("dp", "head")),
        P("tok", ("dp", "head"), None),
        P("tok", None),
        P("tok", None),
        P(None, ("dp", "head")),
        P(),
    )
    return jax.shard_map(
        per_device,
        mesh=mesh,
        in_specs=placed,
        out_specs=P(("groups", "dp", "head"), "tok", None, None),
        check_vma=False,
    )
```

profile of v0, /device:TPU:0, one launch (start us, length us, event | category | flops | bytes accessed | tf_op | source)
XLA Modules:
  0.0 201.4 jit_solution(498799030613453234)
XLA Ops:
  6.5 5.2 %sort.17 = (s32[1024]{0:T(1024)}, s32[1024]{0:T(1024)S(1)}) sort(s32[1024]{0:T(1024)} %param.19, s32[1024]{0:T(1024)S(1)} %iota.4), dimensions={0}, to_apply=%region_0.0 | sort | flops 10240 | bytes 16384 | tf_op jit(solution)/shard_map/jit(argsort)/sort | solution.py:41
  11.8 1.5 convolution_convert_fusion.1
  13.2 20.5 %psum.7 = bf16[16,512]{1,0:T(8,128)(2,1)S(1)} all-reduce(bf16[16,512]{1,0:T(8,128)(2,1)S(1)} %convolution_convert_fusion.1), channel_id=1, replica_groups=mesh['groups'=2,'tok'=4,'dp'=2,'head'=2] {'tok'}, use_global_device_ids=true, to_apply=%region_1.0 | all-reduce | flops 8192 | bytes 32768 | tf_op jit(solution)/shard_map/psum | solution.py:37
  33.7 1.5 fusion.39
  35.4 4.3 %gather_fusion = bf16[1024,16]{1,0:T(8,128)(2,1)} fusion(bf16[16,1024]{0,1:T(8,128)(2,1)S(1)} %copy.24, s32[1024]{0:T(1024)S(1)} %fusion.42), kind=kCustom, calls=%fused_computation | custom fusion | bytes 69632 | tf_op jit(solution)/shard_map/jit(_take)/gather | solution.py:42
  39.7 1.0 copy.25
  40.8 8.0 %all_to_all.36 = bf16[16,4,256]{2,0,1:T(8,128)(2,1)S(1)} all-to-all(bf16[16,4,256]{2,0,1:T(8,128)(2,1)S(1)} %broadcast_select_fusion), channel_id=1, replica_groups=mesh['groups'=2,'tok'=4,'dp'=2,'head'=2] {'tok'}, dimensions={1} | all-to-all | bytes 65536 | tf_op jit(solution)/shard_map/all_to_all | solution.py:43
  49.8 1.3 fusion.16
  51.2 2.4 %copy.27 = bf16[16,8,1536]{0,1,2:T(8,128)(2,1)S(1)} copy(bf16[16,8,1536]{2,0,1:T(8,128)(2,1)S(1)} %fusion.16) | data formatting | bytes 786432 | tf_op jit(solution)/shard_map/convert_element_type | solution.py:53
  53.6 3.9 %reshape.70 = bf16[4,2,24576]{2,1,0:T(2,128)(2,1)} reshape(bf16[1536,8,16]{2,1,0:T(8,128)(2,1)S(1)} %bitcast.75) | data formatting | bytes 786432
  57.5 13.0 %all_to_all.37 = bf16[4,2,24576]{2,1,0:T(2,128)(2,1)} all-to-all(bf16[4,2,24576]{2,1,0:T(2,128)(2,1)} %reshape.70), channel_id=1, replica_groups=mesh['groups'=2,'tok'=4,'dp'=2,'head'=2] {'tok'}, dimensions={0} | all-to-all | bytes 786432 | tf_op jit(solution)/shard_map/all_to_all | solution.py:54
  70.5 3.5 %reshape.71 = bf16[1536,8,16]{2,1,0:T(8,128)(2,1)S(1)} reshape(bf16[4,2,24576]{2,1,0:T(2,128)(2,1)} %all_to_all.37) | data formatting | bytes 786432
  74.0 2.8 %copy.28 = f32[16,8,4,384]{3,1,2,0:T(8,128)} copy(bf16[16,8,4,384]{0,1,3,2:T(8,128)(2,1)S(1)} %bitcast.76) | data formatting | bytes 1179648 | tf_op jit(solution)/shard_map/convert_element_type | solution.py:61
  76.8 1.9 reshape.58
  78.7 1.7 copy.29
  80.5 2.8 %reshape.57 = f32[16,8,1536]{2,0,1:T(8,128)S(1)} reshape(f32[16,8,32,48]{3,2,0,1:T(8,128)} %copy.29) | data formatting | bytes 1572864 | tf_op jit(solution)/shard_map/convert_element_type | solution.py:61
  84.7 18.5 %all-gather.3.cloned.1.call-done = bf16[64,8,1536]{2,0,1:T(8,128)(2,1)} async-done(((bf16[16,8,1536]{2,0,1:T(8,128)(2,1)}), bf16[64,8,1536]{2,0,1:T(8,128)(2,1)}) %all-gather.3.cloned.1.call-update) | async-done | bytes 1572880 | tf_op jit(solution)/shard_map/all_gather | solution.py:63
  103.2 20.0 %fusion.2 = bf16[64,8,1536]{2,0,1:T(8,128)(2,1)} fusion(bf16[8,768,1536]{2,1,0:T(8,128)(2,1)} %param.25, bf16[64,8,1536]{2,0,1:T(8,128)(2,1)} %all-gather.3.cloned.1.call-done, bf16[8,1536,768]{2,1,0:T(8,128)(2,1)} %param.23, f32[8,768]{1,0:T(8,128)S(1)} %copy-done.3), kind=kOutput, calls=%fused_computation.4 | convolution fusion | flops 2420637696 | bytes 40919040 | tf_op jit(solution)/shard_map/rjh,jhd->rjd/dot_general | solution.py:70
  124.0 27.6 %reduce-scatter.2.cloned.1.call-done = bf16[16,8,1536]{2,0,1:T(8,128)(2,1)} async-done(((bf16[64,8,1536]{2,0,1:T(8,128)(2,1)}), bf16[16,8,1536]{2,0,1:T(8,128)(2,1)}) %reduce-scatter.2.cloned.1.call-update) | async-done | bytes 393232 | tf_op jit(solution)/shard_map/reduce_scatter | solution.py:69
  151.6 1.2 multiply_reduce_fusion
  152.8 1.2 multiply_convert_fusion
  154.2 16.1 %all_to_all.38 = bf16[16,8,1536]{2,1,0:T(8,128)(2,1)S(1)} all-to-all(bf16[16,8,1536]{2,1,0:T(8,128)(2,1)S(1)} %copy.30), channel_id=1, replica_groups=mesh['groups'=2,'tok'=4,'dp'=2,'head'=2] {'tok'}, dimensions={0} | all-to-all | bytes 786432 | tf_op jit(solution)/shard_map/all_to_all | solution.py:80
  170.4 20.3 %all-gather.5.cloned.1.call-done = bf16[1536,1536]{1,0:T(8,128)(2,1)} async-done(((bf16[1536,384]{1,0:T(8,128)(2,1)}), bf16[1536,1536]{1,0:T(8,128)(2,1)}) %all-gather.5.cloned.1.call-update) | async-done | bytes 4718608 | tf_op jit(solution)/shard_map/all_gather | solution.py:82
  190.7 4.2 %fusion.26 = bf16[1,4,32,1536]{3,2,1,0:T(8,128)(2,1)} fusion(bf16[1536,1536]{1,0:T(8,128)(2,1)} %all-gather.5.cloned.1.call-done, bf16[4,4,8,1536]{3,2,1,0:T(8,128)(2,1)S(1)} %bitcast.80, f32[1536]{0:T(1024)S(1)} %copy-done.7), kind=kOutput, calls=%fused_computation.16 | convolution fusion | flops 605356032 | bytes 5511168 | tf_op jit(solution)/shard_map/dot_general | solution.py:84
  (36 shorter events, 3.5 us)
Async XLA Ops:
  6.5 43.3 %copy-start = (bf16[8,128,1536]{2,1,0:T(8,128)(2,1)S(1)}, bf16[8,128,1536]{2,1,0:T(8,128)(2,1)}, u32[]{:S(2)}) copy-start(bf16[8,128,1536]{2,1,0:T(8,128)(2,1)} %param.20) | copy-start | bytes 9437188
  6.5 96.7 %all-gather.3.cloned.1.call-start = ((), (), s32[]{:S(2)}) async-start(), calls=%async_computation.4 | async-start | bytes 1966080 | tf_op jit(solution)/shard_map/all_gather | solution.py:63
  80.5 3.0 %copy-start.5 = (f32[8,1536]{1,0:T(8,128)S(1)}, f32[8,1536]{1,0:T(8,128)}, u32[]{:S(2)}) copy-start(f32[8,1536]{1,0:T(8,128)} %param.22) | copy-start | bytes 147460
  83.3 19.9 %copy-start.3 = (f32[8,768]{1,0:T(8,128)S(1)}, f32[8,768]{1,0:T(8,128)}, u32[]{:S(2)}) copy-start(f32[8,768]{1,0:T(8,128)} %param.24) | copy-start | bytes 73732
  84.5 67.1 %reduce-scatter.2.cloned.1.call-start = ((), (), s32[]{:S(2)}) async-start(), calls=%async_computation.5 | async-start | bytes 1966080 | tf_op jit(solution)/shard_map/reduce_scatter | solution.py:69
  123.2 28.4 %copy-start.2 = (bf16[16,8,1536]{2,0,1:T(8,128)(2,1)S(1)}, bf16[16,8,1536]{2,0,1:T(8,128)(2,1)}, u32[]{:S(2)}) copy-start(bf16[16,8,1536]{2,0,1:T(8,128)(2,1)} %multiply_convert_fusion.1) | copy-start | bytes 1179652
  123.2 28.4 %copy-start.4 = (f32[8,1536]{1,0:T(8,128)S(1)}, f32[8,1536]{1,0:T(8,128)}, u32[]{:S(2)}) copy-start(f32[8,1536]{1,0:T(8,128)} %param.26) | copy-start | bytes 147460
  123.2 29.6 %copy-start.6 = (f32[8,1536]{1,0:T(8,128)S(1)}, f32[8,1536]{1,0:T(8,128)}, u32[]{:S(2)}) copy-start(f32[8,1536]{1,0:T(8,128)} %param.27) | copy-start | bytes 147460
  123.2 67.4 %all-gather.5.cloned.1.call-start = ((), (), s32[]{:S(2)}) async-start(), calls=%async_computation.6 | async-start | bytes 5898240 | tf_op jit(solution)/shard_map/all_gather | solution.py:82
  152.8 37.9 %copy-start.7 = (f32[1536]{0:T(1024)S(1)}, f32[1536]{0:T(1024)}, u32[]{:S(2)}) copy-start(f32[1536]{0:T(1024)} %param.29) | copy-start | bytes 18436
  190.7 4.2 %copy-start.1 = (bf16[8,128,1536]{2,1,0:T(8,128)(2,1)S(1)}, bf16[8,128,1536]{2,1,0:T(8,128)(2,1)}, u32[]{:S(2)}) copy-start(bf16[8,128,1536]{2,1,0:T(8,128)(2,1)} %param.20) | copy-start | bytes 9437188
Sparse Core Ops, SparseCore 0:
  84.6 18.5 all-gather.2
  123.4 28.1 reduce-scatter.1
  153.2 37.3 all-gather.4
where the time goes:
time: 202 us; the launch traced here: 201 us
  waiting for transfers between devices  67.1 us (33%)
  blocking collectives  57.7 us (29%)
  matrix products  28.5 us (14%)
  local copies, waits for them, and re-layouts  25.9 us (13%)
  between operations  13.2 us (7%)
  other arithmetic  8.73 us (4%)
    reduce_scatter x1, waiting for transfers between devices, per_device(): lax.psum_scatter(jnp.einsum('rjh,jhd->rjd', activated, contract_weight, p...  27.6 us
    psum x1, blocking collectives, per_device(): low_rank = lax.psum(partial_low.astype(jnp.bfloat16), 'tok')  20.5 us
    all_gather x1, waiting for transfers between devices, per_device(): lax.all_gather(gate_weight, ('dp', 'head'), axis=1, tiled=True)  20.3 us
    dot_general x1, matrix products, per_device(): jnp.einsum('rjh,jhd->rjd', activated, contract_weight, preferred_element_...  20 us
    all_gather x1, waiting for transfers between devices, per_device(): every_row = lax.all_gather(first_norm, ('dp', 'head'), axis=0, tiled=True)  18.5 us
    all_to_all x1, blocking collectives, per_device(): lax.all_to_all(second_norm, 'tok', split_axis=0, concat_axis=1, tiled=True)  16.1 us
    all_to_all x1, blocking collectives, per_device(): lax.all_to_all(embedded, 'tok', split_axis=2, concat_axis=1, tiled=True)  13 us
    convert_element_type x4, local copies, waits for them, and re-layouts, per_device(): mixed_heads.astype(jnp.float32) + embedded.astype(jnp.float32)  9.26 us
  transfers between devices with their start and end apart: 3, of which 3 were waited for; matrix products, arithmetic and copies ran while one was open for 1% of the time, Pallas kernels for 0%

commit v1 on v0

--- a/solution.py
+++ b/solution.py
@@ -1,6 +1,10 @@
+import functools
+
 import jax
 import jax.numpy as jnp
 from jax import lax
+from jax.experimental import pallas as pl
+from jax.experimental.pallas import tpu as pltpu
 from jax.sharding import PartitionSpec as P
 
 FEAT_TOKENS = 32
@@ -12,7 +16,7 @@
     return values * scale * gain_row
 
 
-def per_device(
+def plain_device(
     features,
     cross_down,
     cross_up,
@@ -89,6 +93,411 @@
     return result[None]
 
 
+MESH = pl.DeviceIdType.MESH
+F32 = jnp.float32
+BF16 = jnp.bfloat16
+
+
+def remote(src, dst, send_sem, recv_sem, device):
+    return pltpu.make_async_remote_copy(
+        src_ref=src, dst_ref=dst, send_sem=send_sem, recv_sem=recv_sem,
+        device_id=device, device_id_type=MESH,
+    )
+
+
+def arrived(slot, send_sem, recv_sem, device):
+    remote(slot, slot, send_sem, recv_sem, device).wait_recv()
+
+
+def fused_kernel(
+    toks, dps, heads,
+    feat, cdown, cup, cbias, ftok, pbias, mgain, ebias, cbias2, bgain, gbias,
+    gate_hbm, proj_hbm, exp_hbm, con_hbm,
+    out,
+    proj_v, exp_v, con_v, gate_v,
+    low_buf, route_send, route_buf, picked, emb, head_buf, mixed, rows_v,
+    part, sib_buf, xs_send, xs_buf, norm_rows, norm_send, norm_buf, perm,
+    w_sem, gate_sem, gate_send, gate_recv, low_send, low_recv, rt_send, rt_recv,
+    hd_send, hd_recv, ag_send, ag_recv, fw_send, sib_send, sib_recv, x_send, x_recv,
+    nm_send, nm_recv,
+):
+    t = lax.axis_index("tok")
+    p = lax.axis_index("dp")
+    h = lax.axis_index("head")
+    mine = p * heads + h
+    here = h * dps + p
+    local_tokens, _, dim = proj_v.shape
+    rows_local = feat.shape[0]
+    feats_local = feat.shape[1]
+    wide = dim // toks
+    total_tokens = toks * local_tokens
+    head_size = dim // total_tokens
+    sibling = {"head": 1 - h}
+
+    def tok_at(q):
+        return lax.rem(t + q, toks)
+
+    def dp_at(q):
+        return lax.rem(p + q, dps)
+
+    def proj_copy(j):
+        return pltpu.make_async_copy(proj_hbm.at[j], proj_v.at[j], w_sem.at[0, j])
+
+    def exp_copy(j):
+        return pltpu.make_async_copy(exp_hbm.at[j], exp_v.at[j], w_sem.at[1, j])
+
+    def con_copy(j):
+        return pltpu.make_async_copy(con_hbm.at[j], con_v.at[j], w_sem.at[2, j])
+
+    gate_own = pltpu.make_async_copy(gate_hbm, gate_v.at[mine], gate_sem)
+    gate_own.start()
+    for j in range(local_tokens):
+        proj_copy(j).start()
+    for j in range(local_tokens):
+        exp_copy(j).start()
+        con_copy(j).start()
+
+    barrier = pltpu.get_barrier_semaphore()
+    for q in range(1, toks):
+        pl.semaphore_signal(barrier, inc=1, device_id={"tok": tok_at(q)}, device_id_type=MESH)
+    for q in range(1, dps):
+        pl.semaphore_signal(barrier, inc=1, device_id={"dp": dp_at(q)}, device_id_type=MESH)
+    pl.semaphore_signal(barrier, inc=1, device_id=sibling, device_id_type=MESH)
+
+    low_buf[t] = jnp.dot(feat[...], cdown[...], preferred_element_type=F32)
+    pl.semaphore_wait(barrier, toks - 1 + dps - 1 + 1)
+
+    def low_copy(q):
+        return remote(low_buf.at[t], low_buf.at[t], low_send.at[q], low_recv.at[t], {"tok": tok_at(q)})
+
+    for q in range(1, toks):
+        low_copy(q).start()
+
+    gate_own.wait()
+
+    def gate_copy(q):
+        slot = gate_v.at[mine]
+        device = sibling if q == 0 else {"dp": dp_at(q)}
+        return remote(slot, slot, gate_send.at[q], gate_recv.at[mine], device)
+
+    def gate_forward(q):
+        source = dp_at(q) * heads + h
+        slot = gate_v.at[source]
+        return remote(slot, slot, gate_send.at[dps + q], gate_recv.at[source], sibling)
+
+    for q in range(dps):
+        gate_copy(q).start()
+
+    lanes = 128
+    share = feats_local // total_tokens
+    feature_at = lax.broadcasted_iota(jnp.int32, (lanes, lanes), 0)
+    feature_of = lax.broadcasted_iota(jnp.int32, (lanes, lanes), 1)
+    place_at = lax.broadcasted_iota(jnp.int32, (feats_local, lanes), 0)
+    per_block = lanes // total_tokens
+    for b in range(feats_local // lanes):
+        token_row = ftok[b : b + 1, :]
+        across = jnp.broadcast_to(token_row, (lanes, lanes))
+        along = across.astype(F32).T.astype(jnp.int32)
+        earlier = jnp.logical_and(across == along, feature_at < feature_of)
+        rank = jnp.sum(jnp.where(earlier, 1.0, 0.0), axis=0, keepdims=True).astype(jnp.int32)
+        place = token_row * share + b * per_block + rank
+        perm[:, b * lanes : (b + 1) * lanes] = jnp.where(place_at == place, 1.0, 0.0).astype(BF16)
+
+    for q in range(1, toks):
+        source = tok_at(q)
+        arrived(low_buf.at[source], low_send.at[q], low_recv.at[source], {"tok": source})
+    low = low_buf[0]
+    for s in range(1, toks):
+        low = low + low_buf[s]
+    lifted = jnp.dot(low.astype(BF16), cup[...], preferred_element_type=F32)
+    widened = feat[...].astype(F32)
+    crossed = (widened * (lifted + cbias[...]) + widened).astype(BF16)
+    grouped = lax.dot_general(
+        crossed, perm[...], (((1,), (1,)), ((), ())), preferred_element_type=F32
+    ).astype(BF16)
+    span = feats_local // toks
+    for s in range(toks):
+        route_send[s] = grouped[:, s * span : (s + 1) * span]
+
+    def route_copy(q):
+        target = tok_at(q)
+        return remote(route_send.at[target], route_buf.at[t], rt_send.at[q], rt_recv.at[t], {"tok": target})
+
+    for q in range(1, toks):
+        route_copy(q).start()
+    route_buf[t] = route_send[t]
+    for q in range(1, toks):
+        source = tok_at(q)
+        arrived(route_buf.at[source], rt_send.at[q], rt_recv.at[source], {"tok": source})
+    for s in range(toks):
+        for j in range(local_tokens):
+            picked[j, :, s * share : (s + 1) * share] = route_buf[s, :, j * share : (j + 1) * share]
+
+    def embed(j, carry):
+        proj_copy(j).wait()
+        value = jnp.dot(picked[j], proj_v[j], preferred_element_type=F32) + pbias[pl.ds(j, 1), :]
+        value = value.astype(BF16)
+        for s in range(toks):
+            emb[s, j] = value[:, s * wide : (s + 1) * wide]
+        return carry
+
+    lax.fori_loop(0, local_tokens, embed, 0)
+
+    def head_copy(q):
+        target = tok_at(q)
+        return remote(emb.at[target], head_buf.at[t], hd_send.at[q], hd_recv.at[t], {"tok": target})
+
+    for q in range(1, toks):
+        head_copy(q).start()
+    head_buf[t] = emb[t]
+
+    def turn(q, carry):
+        source = tok_at(q)
+
+        @pl.when(q > 0)
+        def _():
+            arrived(head_buf.at[source], hd_send.at[q], hd_recv.at[source], {"tok": source})
+
+        for i in range(local_tokens):
+            for k in range(local_tokens):
+                mixed[source, k, :, i * head_size : (i + 1) * head_size] = head_buf[
+                    source, i, :, k * head_size : (k + 1) * head_size
+                ]
+        return carry
+
+    lax.fori_loop(0, toks, turn, 0)
+
+    def gather_copy(j, q):
+        slot = rows_v.at[j, here]
+        device = sibling if q == 0 else {"dp": dp_at(q)}
+        return remote(slot, slot, ag_send.at[j, q], ag_recv.at[j, here], device)
+
+    def gather_forward(j, q):
+        source = h * dps + dp_at(q)
+        slot = rows_v.at[j, source]
+        return remote(slot, slot, fw_send.at[j, q], ag_recv.at[j, source], sibling)
+
+    def first(j, carry):
+        sums = []
+        square = jnp.zeros((rows_local, 1), F32)
+        for s in range(toks):
+            value = mixed[s, j].astype(F32) + emb[s, j].astype(F32)
+            sums.append(value)
+            square = square + jnp.sum(value * value, axis=1, keepdims=True)
+        scale = lax.rsqrt(square * (1.0 / dim) + 1e-06)
+        for s in range(toks):
+            gain = mgain[pl.ds(j, 1), s * wide : (s + 1) * wide]
+            rows_v[j, here, :, s * wide : (s + 1) * wide] = (sums[s] * scale * gain).astype(BF16)
+        for q in range(dps):
+            gather_copy(j, q).start()
+        return carry
+
+    lax.fori_loop(0, local_tokens, first, 0)
+
+    def forward(j):
+        for q in range(1, dps):
+            source = h * dps + dp_at(q)
+            arrived(rows_v.at[j, source], fw_send.at[j, q], ag_recv.at[j, source], sibling)
+            gather_forward(j, q).start()
+
+    def pair_copy(j):
+        return remote(part.at[j, 1 - h], sib_buf.at[j], sib_send.at[j], sib_recv.at[j], sibling)
+
+    def network(j):
+        for q in range(dps):
+            source = (1 - h) * dps + dp_at(q)
+            arrived(rows_v.at[j, source], fw_send.at[j, q], ag_recv.at[j, source], sibling)
+        exp_copy(j).wait()
+        con_copy(j).wait()
+        everything = rows_v[j].reshape(heads * dps * rows_local, dim)
+        inner = jnp.dot(everything, exp_v[j], preferred_element_type=F32) + ebias[pl.ds(j, 1), :]
+        active = jax.nn.gelu(inner).astype(BF16)
+        sums = jnp.dot(active, con_v[j], preferred_element_type=F32).astype(BF16)
+        part[j] = sums.reshape(heads, dps, rows_local, dim)
+        pair_copy(j).start()
+
+    def cross_copy(j, q):
+        return remote(
+            xs_send.at[j, q - 1], xs_buf.at[j, q - 1], x_send.at[j, q], x_recv.at[j, q], {"dp": dp_at(q)}
+        )
+
+    def combine(j):
+        arrived(sib_buf.at[j], sib_send.at[j], sib_recv.at[j], sibling)
+        for q in range(1, dps):
+            target = dp_at(q)
+            both = part[j, h, target].astype(F32) + sib_buf[j, target].astype(F32)
+            xs_send[j, q - 1] = both.astype(BF16)
+            cross_copy(j, q).start()
+
+    def finish(j):
+        total = part[j, h, p].astype(F32) + sib_buf[j, p].astype(F32)
+        for q in range(1, dps):
+            arrived(xs_buf.at[j, q - 1], x_send.at[j, q], x_recv.at[j, q], sibling)
+            total = total + xs_buf[j, q - 1].astype(F32)
+        total = total + cbias2[pl.ds(j, 1), :] + rows_v[j, here].astype(F32)
+        scale = lax.rsqrt(jnp.sum(total * total, axis=1, keepdims=True) * (1.0 / dim) + 1e-06)
+        value = total * scale * bgain[pl.ds(j, 1), :]
+        for r in range(rows_local):
+            norm_rows[r, pl.ds(j, 1), :] = value[r : r + 1, :]
+
+    def step(i, carry):
+        @pl.when(i < local_tokens)
+        def _():
+            forward(i)
+
+        @pl.when(jnp.logical_and(i >= 1, i < local_tokens + 1))
+        def _():
+            network(i - 1)
+
+        @pl.when(jnp.logical_and(i >= 2, i < local_tokens + 2))
+        def _():
+            combine(i - 2)
+
+        @pl.when(i >= 4)
+        def _():
+            finish(i - 4)
+
+        return carry
+
+    lax.fori_loop(0, local_tokens + 4, step, 0)
+
+    for q in range(1, dps):
+        source = dp_at(q) * heads + h
+        arrived(gate_v.at[source], gate_send.at[q], gate_recv.at[source], sibling)
+        gate_forward(q).start()
+
+    split_rows = rows_local // toks
+    block = split_rows * local_tokens
+    for s in range(toks):
+        norm_send[s] = (
+            norm_rows[s * split_rows : (s + 1) * split_rows].reshape(block, dim).astype(BF16)
+        )
+
+    def norm_copy(q):
+        target = tok_at(q)
+        return remote(norm_send.at[target], norm_buf.at[t], nm_send.at[q], nm_recv.at[t], {"tok": target})
+
+    for q in range(1, toks):
+        norm_copy(q).start()
+    norm_buf[t] = norm_send[t]
+    for q in range(dps):
+        source = dp_at(q) * heads + (1 - h)
+        arrived(gate_v.at[source], gate_send.at[q], gate_recv.at[source], sibling)
+    for q in range(1, toks):
+        source = tok_at(q)
+        arrived(norm_buf.at[source], nm_send.at[q], nm_recv.at[source], {"tok": source})
+
+    states = norm_buf[...].reshape(toks * block, dim)
+    columns = gate_v.shape[2]
+    for c in range(dps * heads):
+        cut = slice(c * columns, (c + 1) * columns)
+        logits = jnp.dot(states, gate_v[c], preferred_element_type=F32) + gbias[:, cut]
+        kept = norm_buf[:, :, cut].reshape(toks * block, columns).astype(F32)
+        gated = (kept * jax.nn.sigmoid(logits)).reshape(toks, split_rows, local_tokens, columns)
+        for r in range(split_rows):
+            out[0, r, :, cut] = gated[:, r].reshape(total_tokens, columns).astype(BF16)
+
+    for q in range(1, toks):
+        low_copy(q).wait_send()
+        route_copy(q).wait_send()
+        head_copy(q).wait_send()
+        norm_copy(q).wait_send()
+    for q in range(dps):
+        gate_copy(q).wait_send()
+    for q in range(1, dps):
+        gate_forward(q).wait_send()
+
+    def drain(j, carry):
+        for q in range(dps):
+            gather_copy(j, q).wait_send()
+        for q in range(1, dps):
+            gather_forward(j, q).wait_send()
+            cross_copy(j, q).wait_send()
+        pair_copy(j).wait_send()
+        return carry
+
+    lax.fori_loop(0, local_tokens, drain, 0)
+
+
+def fused_device(
+    features, cross_down, cross_up, cross_bias, feature_token, proj_weight, proj_bias,
+    mix_gain, expand_weight, expand_bias, contract_weight, contract_bias, block_gain,
+    gate_weight, gate_bias,
+):
+    toks, dps, heads = lax.axis_size("tok"), lax.axis_size("dp"), lax.axis_size("head")
+    rows, feats = features.shape
+    local, token_feats, dim = proj_weight.shape
+    hidden = expand_weight.shape[2]
+    wide = dim // toks
+    split_rows = rows // toks
+    block = split_rows * local
+    vmem = pl.BlockSpec(memory_space=pltpu.VMEM)
+    anywhere = pl.BlockSpec(memory_space=pl.ANY)
+    dma = pltpu.SemaphoreType.DMA
+    slots = heads * dps
+    scratch = [
+        pltpu.VMEM((local, token_feats, dim), BF16),
+        pltpu.VMEM((local, dim, hidden), BF16),
+        pltpu.VMEM((local, hidden, dim), BF16),
+        pltpu.VMEM((slots,) + gate_weight.shape, BF16),
+        pltpu.VMEM((toks, rows, cross_down.shape[1]), F32),
+        pltpu.VMEM((toks, rows, feats // toks), BF16),
+        pltpu.VMEM((toks, rows, feats // toks), BF16),
+        pltpu.VMEM((local, rows, token_feats), BF16),
+        pltpu.VMEM((toks, local, rows, wide), BF16),
+        pltpu.VMEM((toks, local, rows, wide), BF16),
+        pltpu.VMEM((toks, local, rows, wide), BF16),
+        pltpu.VMEM((local, slots, rows, dim), BF16),
+        pltpu.VMEM((local, heads, dps, rows, dim), BF16),
+        pltpu.VMEM((local, dps, rows, dim), BF16),
+        pltpu.VMEM((local, dps - 1, rows, dim), BF16),
+        pltpu.VMEM((local, dps - 1, rows, dim), BF16),
+        pltpu.VMEM((rows, local, dim), F32),
+        pltpu.VMEM((toks, block, dim), BF16),
+        pltpu.VMEM((toks, block, dim), BF16),
+        pltpu.VMEM((feats, feats), BF16),
+        dma((3, local)), dma, dma((2 * dps,)), dma((slots,)),
+        dma((toks,)), dma((toks,)), dma((toks,)), dma((toks,)),
+        dma((toks,)), dma((toks,)),
+        dma((local, dps)), dma((local, slots)), dma((local, dps)),
+        dma((local,)), dma((local,)), dma((local, dps)), dma((local, dps)),
+        dma((toks,)), dma((toks,)),
+    ]
+    return pl.pallas_call(
+        functools.partial(fused_kernel, toks, dps, heads),
+        out_shape=jax.ShapeDtypeStruct((1, split_rows, toks * local, dim), BF16),
+        in_specs=[vmem] * 11 + [anywhere] * 4,
+        out_specs=vmem,
+        scratch_shapes=scratch,
+        compiler_params=pltpu.CompilerParams(
+            collective_id=0, has_side_effects=True, vmem_limit_bytes=63 * 2**20
+        ),
+    )(
+        features, cross_down, cross_up, cross_bias.reshape(1, -1),
+        feature_token.reshape(-1, 128), proj_bias, mix_gain, expand_bias, contract_bias,
+        block_gain, gate_bias.reshape(1, -1), gate_weight, proj_weight, expand_weight,
+        contract_weight,
+    )
+
+
+def per_device(*arrays):
+    features, gate_weight = arrays[0], arrays[13]
+    toks = lax.axis_size("tok")
+    local = arrays[5].shape[0]
+    fits = (
+        lax.axis_size("head") == 2
+        and lax.axis_size("dp") > 1
+        and (DIM // toks) % 128 == 0
+        and gate_weight.shape[1] % 128 == 0
+        and features.shape[0] % 16 == 0
+        and features.shape[0] % toks == 0
+        and (features.shape[1] // toks) % 128 == 0
+        and features.shape[0] // toks * local % 16 == 0
+        and local % 8 == 0
+    )
+    return (fused_device if fits else plain_device)(*arrays)
+
+
 def solution(mesh):
     placed = (
         P(("groups", "dp", "head"), "tok"),

time: 202 us -> 80.3 us (0.40)
  Pallas kernels: 0 us -> 77 us
  waiting for transfers between devices: 67.1 us -> 0 us
  blocking collectives: 57.7 us -> 0 us
  matrix products: 28.5 us -> 0 us
  local copies, waits for them, and re-layouts: 25.9 us -> 3.06 us
  between operations: 13.2 us -> 0.01 us
  other arithmetic: 8.73 us -> 0 us
    pallas_call x0 -> x1, Pallas kernels: none -> 77 us  [fused_device(): pl.pallas_call(functools.partial(fused_kernel, toks, dps, heads), out_sha...]
    all_gather x2 -> x0, waiting for transfers between devices: 38.8 us -> none  [the longest x1 20.3 us: per_device(): lax.all_gather(gate_weight, ('dp', 'head'), axis=1, tiled=True)]
    all_to_all x3 -> x0, blocking collectives: 37.2 us -> none  [the longest x1 16.1 us: per_device(): lax.all_to_all(second_norm, 'tok', split_axis=0, concat_axis=1, tiled=True)]
    dot_general x5 -> x0, matrix products: 28.5 us -> none  [the longest x1 20 us: per_device(): jnp.einsum('rjh,jhd->rjd', activated, contract_weight, preferred_element_...]
    reduce_scatter x1 -> x0, waiting for transfers between devices: 27.6 us -> none  [per_device(): lax.psum_scatter(jnp.einsum('rjh,jhd->rjd', activated, contract_weight, p...]
    psum x1 -> x0, blocking collectives: 20.5 us -> none  [per_device(): low_rank = lax.psum(partial_low.astype(jnp.bfloat16), 'tok')]
    convert_element_type x7 -> x0, local copies, waits for them, and re-layouts: 12.1 us -> none  [the longest x4 9.26 us: per_device(): mixed_heads.astype(jnp.float32) + embedded.astype(jnp.float32)]
    unnamed x18 -> x1, local copies, waits for them, and re-layouts: 7.45 us -> 1.77 us
  transfers between devices with their start and end apart: 3 -> 0, of which waited for: 3 -> 0; matrix products, arithmetic and copies ran while one was open for 1% -> 0% of each run, Pallas kernels for 0% -> 0%
where the time goes in v1:
time: 80.3 us; the launch traced here: 80.1 us
  Pallas kernels  77 us (96%)
  local copies, waits for them, and re-layouts  3.06 us (4%)
    pallas_call x1, Pallas kernels, fused_device(): pl.pallas_call(functools.partial(fused_kernel, toks, dps, heads), out_sha...  77 us
    unnamed x1, local copies, waits for them, and re-layouts  1.77 us

profile of v1, /device:TPU:0, one launch (start us, length us, event | category | flops | bytes accessed | tf_op | source)
XLA Modules:
  0.0 80.1 jit_solution(16359911519995589261)
XLA Ops:
  0.0 1.3 %reshape.11.gbias = f32[1,1536]{1,0:T(1,128)} reshape(f32[1536]{0:T(1024)} %param.29) | data formatting | bytes 12288 | tf_op jit(solution)/shard_map/reshape | solution.py:478
  1.3 77.0 %shard_map.145 = bf16[1,4,32,1536]{3,2,1,0:T(8,128)(2,1)} custom-call(bf16[16,1024]{1,0:T(8,128)(2,1)} %feat.1, bf16[1024,512]{1,0:T(8,128)(2,1)} %cdown.1, bf16[512,1024]{1,0:T(8,128)(2,1)} %cup.1, f32[1,1024]{1,0:T(1,128)} %bitcast.2, s32[8,128]{1,0:T(8,128)} %bitcast.3, f32[8,1536]{1,0:T(8,128)} %pbias.1, f32[8,1536]{1,0:T(8,128)} %mgain.1, ...), custom_call_target="tpu_custom_call" | custom-call | tf_op jit(solution)/shard_map/pallas_call | solution.py:466
  78.3 1.8 %copy.17 = bf16[1,4,32,1536]{3,2,1,0:T(8,128)(2,1)} copy(bf16[1,4,32,1536]{3,2,1,0:T(8,128)(2,1)} %shard_map.145) | data formatting | bytes 786432

commit v2 on v1

--- a/solution.py
+++ b/solution.py
@@ -124,6 +124,7 @@
     t = lax.axis_index("tok")
     p = lax.axis_index("dp")
     h = lax.axis_index("head")
+    u = lax.axis_index("groups")
     mine = p * heads + h
     here = h * dps + p
     local_tokens, _, dim = proj_v.shape
@@ -133,6 +134,7 @@
     total_tokens = toks * local_tokens
     head_size = dim // total_tokens
     sibling = {"head": 1 - h}
+    replica = {"groups": 1 - u}
 
     def tok_at(q):
         return lax.rem(t + q, toks)
@@ -153,9 +155,6 @@
     gate_own.start()
     for j in range(local_tokens):
         proj_copy(j).start()
-    for j in range(local_tokens):
-        exp_copy(j).start()
-        con_copy(j).start()
 
     barrier = pltpu.get_barrier_semaphore()
     for q in range(1, toks):
@@ -163,9 +162,10 @@
     for q in range(1, dps):
         pl.semaphore_signal(barrier, inc=1, device_id={"dp": dp_at(q)}, device_id_type=MESH)
     pl.semaphore_signal(barrier, inc=1, device_id=sibling, device_id_type=MESH)
+    pl.semaphore_signal(barrier, inc=1, device_id=replica, device_id_type=MESH)
 
     low_buf[t] = jnp.dot(feat[...], cdown[...], preferred_element_type=F32)
-    pl.semaphore_wait(barrier, toks - 1 + dps - 1 + 1)
+    pl.semaphore_wait(barrier, toks - 1 + dps - 1 + 2)
 
     def low_copy(q):
         return remote(low_buf.at[t], low_buf.at[t], low_send.at[q], low_recv.at[t], {"tok": tok_at(q)})
@@ -176,14 +176,21 @@
     gate_own.wait()
 
     def gate_copy(q):
-        slot = gate_v.at[mine]
-        device = sibling if q == 0 else {"dp": dp_at(q)}
-        return remote(slot, slot, gate_send.at[q], gate_recv.at[mine], device)
-
-    def gate_forward(q):
+        if q == 0:
+            slot = gate_v.at[mine]
+            return remote(slot, slot, gate_send.at[0, q], gate_recv.at[mine, 0], sibling)
+        slot = gate_v.at[mine, u]
+        return remote(slot, slot, gate_send.at[0, q], gate_recv.at[mine, u], {"dp": dp_at(q)})
+
+    def gate_forward(q, kind):
         source = dp_at(q) * heads + h
-        slot = gate_v.at[source]
-        return remote(slot, slot, gate_send.at[dps + q], gate_recv.at[source], sibling)
+        half = 1 - u if kind == 3 else u
+        device = replica if kind == 1 else sibling
+        slot = gate_v.at[source, half]
+        return remote(slot, slot, gate_send.at[kind, q], gate_recv.at[source, half], device)
+
+    def gate_arrived(source, half):
+        arrived(gate_v.at[source, half], gate_send.at[0, 0], gate_recv.at[source, half], sibling)
 
     for q in range(dps):
         gate_copy(q).start()
@@ -226,6 +233,9 @@
     for q in range(1, toks):
         route_copy(q).start()
     route_buf[t] = route_send[t]
+    for j in range(local_tokens):
+        exp_copy(j).start()
+        con_copy(j).start()
     for q in range(1, toks):
         source = tok_at(q)
         arrived(route_buf.at[source], rt_send.at[q], rt_recv.at[source], {"tok": source})
@@ -266,6 +276,10 @@
         return carry
 
     lax.fori_loop(0, toks, turn, 0)
+    for q in range(1, dps):
+        gate_arrived(dp_at(q) * heads + h, u)
+        gate_forward(q, 1).start()
+        gate_forward(q, 2).start()
 
     def gather_copy(j, q):
         slot = rows_v.at[j, here]
@@ -362,9 +376,8 @@
     lax.fori_loop(0, local_tokens + 4, step, 0)
 
     for q in range(1, dps):
-        source = dp_at(q) * heads + h
-        arrived(gate_v.at[source], gate_send.at[q], gate_recv.at[source], sibling)
-        gate_forward(q).start()
+        gate_arrived(dp_at(q) * heads + h, 1 - u)
+        gate_forward(q, 3).start()
 
     split_rows = rows_local // toks
     block = split_rows * local_tokens
@@ -380,18 +393,21 @@
     for q in range(1, toks):
         norm_copy(q).start()
     norm_buf[t] = norm_send[t]
-    for q in range(dps):
-        source = dp_at(q) * heads + (1 - h)
-        arrived(gate_v.at[source], gate_send.at[q], gate_recv.at[source], sibling)
+    beside = gate_v.at[p * heads + (1 - h)]
+    arrived(beside, gate_send.at[0, 0], gate_recv.at[p * heads + (1 - h), 0], sibling)
+    for q in range(1, dps):
+        for half in range(2):
+            gate_arrived(dp_at(q) * heads + (1 - h), half)
     for q in range(1, toks):
         source = tok_at(q)
         arrived(norm_buf.at[source], nm_send.at[q], nm_recv.at[source], {"tok": source})
 
+    gate_row = gbias[...].reshape(1, dim)
     states = norm_buf[...].reshape(toks * block, dim)
-    columns = gate_v.shape[2]
+    columns = gate_v.shape[3]
     for c in range(dps * heads):
         cut = slice(c * columns, (c + 1) * columns)
-        logits = jnp.dot(states, gate_v[c], preferred_element_type=F32) + gbias[:, cut]
+        logits = jnp.dot(states, gate_v[c].reshape(dim, columns), preferred_element_type=F32) + gate_row[:, cut]
         kept = norm_buf[:, :, cut].reshape(toks * block, columns).astype(F32)
         gated = (kept * jax.nn.sigmoid(logits)).reshape(toks, split_rows, local_tokens, columns)
         for r in range(split_rows):
@@ -405,7 +421,8 @@
     for q in range(dps):
         gate_copy(q).wait_send()
     for q in range(1, dps):
-        gate_forward(q).wait_send()
+        for kind in range(1, 4):
+            gate_forward(q, kind).wait_send()
 
     def drain(j, carry):
         for q in range(dps):
@@ -439,7 +456,7 @@
         pltpu.VMEM((local, token_feats, dim), BF16),
         pltpu.VMEM((local, dim, hidden), BF16),
         pltpu.VMEM((local, hidden, dim), BF16),
-        pltpu.VMEM((slots,) + gate_weight.shape, BF16),
+        pltpu.VMEM((slots, 2, dim // 2, gate_weight.shape[1]), BF16),
         pltpu.VMEM((toks, rows, cross_down.shape[1]), F32),
         pltpu.VMEM((toks, rows, feats // toks), BF16),
         pltpu.VMEM((toks, rows, feats // toks), BF16),
@@ -456,13 +473,14 @@
         pltpu.VMEM((toks, block, dim), BF16),
         pltpu.VMEM((toks, block, dim), BF16),
         pltpu.VMEM((feats, feats), BF16),
-        dma((3, local)), dma, dma((2 * dps,)), dma((slots,)),
+        dma((3, local)), dma, dma((4, dps)), dma((slots, 2)),
         dma((toks,)), dma((toks,)), dma((toks,)), dma((toks,)),
         dma((toks,)), dma((toks,)),
         dma((local, dps)), dma((local, slots)), dma((local, dps)),
         dma((local,)), dma((local,)), dma((local, dps)), dma((local, dps)),
         dma((toks,)), dma((toks,)),
     ]
+    gate_halves = gate_weight.reshape(2, -1, gate_weight.shape[1])
     return pl.pallas_call(
         functools.partial(fused_kernel, toks, dps, heads),
         out_shape=jax.ShapeDtypeStruct((1, split_rows, toks * local, dim), BF16),
@@ -475,7 +493,7 @@
     )(
         features, cross_down, cross_up, cross_bias.reshape(1, -1),
         feature_token.reshape(-1, 128), proj_bias, mix_gain, expand_bias, contract_bias,
-        block_gain, gate_bias.reshape(1, -1), gate_weight, proj_weight, expand_weight,
+        block_gain, gate_bias, gate_halves, proj_weight, expand_weight,
         contract_weight,
     )
 
@@ -486,6 +504,7 @@
     local = arrays[5].shape[0]
     fits = (
         lax.axis_size("head") == 2
+        and lax.axis_size("groups") == 2
         and lax.axis_size("dp") > 1
         and (DIM // toks) % 128 == 0
         and gate_weight.shape[1] % 128 == 0

time: 80.3 us -> 61 us (0.76)
  the two profiles are of different devices: /device:TPU:0 before, /device:TPU:28 now
where the time goes in v2:
time: 61 us; the launch traced here: 60.8 us
  Pallas kernels  59 us (97%)
  local copies, waits for them, and re-layouts  1.77 us (3%)
    pallas_call x1, Pallas kernels, fused_device(): pl.pallas_call(functools.partial(fused_kernel, toks, dps, heads), out_sha...  59 us
    unnamed x1, local copies, waits for them, and re-layouts  1.77 us

profile of v2, /device:TPU:28, one launch (start us, length us, event | category | flops | bytes accessed | tf_op | source)
XLA Modules:
  0.0 60.8 jit_solution(8691281071623794701)
XLA Ops:
  0.0 59.0 %shard_map.145 = bf16[1,4,32,1536]{3,2,1,0:T(8,128)(2,1)} custom-call(bf16[16,1024]{1,0:T(8,128)(2,1)} %feat.1, bf16[1024,512]{1,0:T(8,128)(2,1)} %cdown.1, bf16[512,1024]{1,0:T(8,128)(2,1)} %cup.1, f32[1,1024]{1,0:T(1,128)} %bitcast.4, s32[8,128]{1,0:T(8,128)} %bitcast.5, f32[8,1536]{1,0:T(8,128)} %pbias.1, f32[8,1536]{1,0:T(8,128)} %mgain.1, ...), custom_call_target="tpu_custom_call" | custom-call | tf_op jit(solution)/shard_map/pallas_call | solution.py:484
  59.0 1.8 %copy.17 = bf16[1,4,32,1536]{3,2,1,0:T(8,128)(2,1)} copy(bf16[1,4,32,1536]{3,2,1,0:T(8,128)(2,1)} %shard_map.145) | data formatting | bytes 786432

commit v3 on v2

--- a/solution.py
+++ b/solution.py
@@ -253,29 +253,31 @@
 
     lax.fori_loop(0, local_tokens, embed, 0)
 
-    def head_copy(q):
+    chunk = 2
+    chunks = local_tokens // chunk
+
+    def head_copy(q, c):
         target = tok_at(q)
-        return remote(emb.at[target], head_buf.at[t], hd_send.at[q], hd_recv.at[t], {"tok": target})
-
-    for q in range(1, toks):
-        head_copy(q).start()
-    head_buf[t] = emb[t]
-
-    def turn(q, carry):
-        source = tok_at(q)
-
-        @pl.when(q > 0)
-        def _():
-            arrived(head_buf.at[source], hd_send.at[q], hd_recv.at[source], {"tok": source})
-
-        for i in range(local_tokens):
-            for k in range(local_tokens):
-                mixed[source, k, :, i * head_size : (i + 1) * head_size] = head_buf[
-                    source, i, :, k * head_size : (k + 1) * head_size
-                ]
-        return carry
-
-    lax.fori_loop(0, toks, turn, 0)
+        cut = pl.ds(c * chunk, chunk)
+        return remote(
+            head_buf.at[target, cut], mixed.at[t, cut], hd_send.at[q, c], hd_recv.at[t, c], {"tok": target}
+        )
+
+    for c in range(chunks):
+
+        def turn(target, carry):
+            for k in range(c * chunk, (c + 1) * chunk):
+                for i in range(local_tokens):
+                    head_buf[target, k, :, i * head_size : (i + 1) * head_size] = emb[
+                        target, i, :, k * head_size : (k + 1) * head_size
+                    ]
+            return carry
+
+        lax.fori_loop(0, toks, turn, 0)
+        for q in range(1, toks):
+            head_copy(q, c).start()
+    mixed[t] = head_buf[t]
+
     for q in range(1, dps):
         gate_arrived(dp_at(q) * heads + h, u)
         gate_forward(q, 1).start()
@@ -306,7 +308,12 @@
             gather_copy(j, q).start()
         return carry
 
-    lax.fori_loop(0, local_tokens, first, 0)
+    for c in range(chunks):
+        for q in range(1, toks):
+            source = tok_at(q)
+            slot = mixed.at[source, pl.ds(c * chunk, chunk)]
+            arrived(slot, hd_send.at[q, c], hd_recv.at[source, c], {"tok": source})
+        lax.fori_loop(c * chunk, (c + 1) * chunk, first, 0)
 
     def forward(j):
         for q in range(1, dps):
@@ -416,7 +423,8 @@
     for q in range(1, toks):
         low_copy(q).wait_send()
         route_copy(q).wait_send()
-        head_copy(q).wait_send()
+        for c in range(chunks):
+            head_copy(q, c).wait_send()
         norm_copy(q).wait_send()
     for q in range(dps):
         gate_copy(q).wait_send()
@@ -475,7 +483,7 @@
         pltpu.VMEM((feats, feats), BF16),
         dma((3, local)), dma, dma((4, dps)), dma((slots, 2)),
         dma((toks,)), dma((toks,)), dma((toks,)), dma((toks,)),
-        dma((toks,)), dma((toks,)),
+        dma((toks, local // 2)), dma((toks, local // 2)),
         dma((local, dps)), dma((local, slots)), dma((local, dps)),
         dma((local,)), dma((local,)), dma((local, dps)), dma((local, dps)),
         dma((toks,)), dma((toks,)),

time: 61 us -> 57.2 us (0.938)
  the two profiles are of different devices: /device:TPU:28 before, /device:TPU:0 now
where the time goes in v3:
time: 57.2 us; the launch traced here: 57 us
  Pallas kernels  55.2 us (97%)
  local copies, waits for them, and re-layouts  1.77 us (3%)
    pallas_call x1, Pallas kernels, fused_device(): pl.pallas_call(functools.partial(fused_kernel, toks, dps, heads), out_sha...  55.2 us
    unnamed x1, local copies, waits for them, and re-layouts  1.77 us

profile of v3, /device:TPU:0, one launch (start us, length us, event | category | flops | bytes accessed | tf_op | source)
XLA Modules:
  0.0 57.0 jit_solution(11118039197271299922)
XLA Ops:
  0.0 55.2 %shard_map.145 = bf16[1,4,32,1536]{3,2,1,0:T(8,128)(2,1)} custom-call(bf16[16,1024]{1,0:T(8,128)(2,1)} %feat.1, bf16[1024,512]{1,0:T(8,128)(2,1)} %cdown.1, bf16[512,1024]{1,0:T(8,128)(2,1)} %cup.1, f32[1,1024]{1,0:T(1,128)} %bitcast.4, s32[8,128]{1,0:T(8,128)} %bitcast.5, f32[8,1536]{1,0:T(8,128)} %pbias.1, f32[8,1536]{1,0:T(8,128)} %mgain.1, ...), custom_call_target="tpu_custom_call" | custom-call | tf_op jit(solution)/shard_map/pallas_call | solution.py:492
  55.2 1.8 %copy.17 = bf16[1,4,32,1536]{3,2,1,0:T(8,128)(2,1)} copy(bf16[1,4,32,1536]{3,2,1,0:T(8,128)(2,1)} %shard_map.145) | data formatting | bytes 786432

commit v4 on v3

--- a/solution.py
+++ b/solution.py
@@ -116,7 +116,7 @@
     out,
     proj_v, exp_v, con_v, gate_v,
     low_buf, route_send, route_buf, picked, emb, head_buf, mixed, rows_v,
-    part, sib_buf, xs_send, xs_buf, norm_rows, norm_send, norm_buf, perm,
+    part, sib_buf, xs_send, xs_buf, norm_rows, norm_send, norm_buf, perm, result,
     w_sem, gate_sem, gate_send, gate_recv, low_send, low_recv, rt_send, rt_recv,
     hd_send, hd_recv, ag_send, ag_recv, fw_send, sib_send, sib_recv, x_send, x_recv,
     nm_send, nm_recv,
@@ -350,6 +350,23 @@
             xs_send[j, q - 1] = both.astype(BF16)
             cross_copy(j, q).start()
 
+    split_rows = rows_local // toks
+    group = norm_buf.shape[2] // split_rows
+    groups_local = local_tokens // group
+
+    def norm_copy(q, k):
+        target = tok_at(q)
+        return remote(
+            norm_send.at[target, k], norm_buf.at[t, k], nm_send.at[q, k], nm_recv.at[t, k], {"tok": target}
+        )
+
+    def leave(k):
+        for s in range(toks):
+            norm_send[s, k] = norm_rows[k, s].astype(BF16)
+        for q in range(1, toks):
+            norm_copy(q, k).start()
+        norm_buf[t, k] = norm_send[t, k]
+
     def finish(j):
         total = part[j, h, p].astype(F32) + sib_buf[j, p].astype(F32)
         for q in range(1, dps):
@@ -359,7 +376,8 @@
         scale = lax.rsqrt(jnp.sum(total * total, axis=1, keepdims=True) * (1.0 / dim) + 1e-06)
         value = total * scale * bgain[pl.ds(j, 1), :]
         for r in range(rows_local):
-            norm_rows[r, pl.ds(j, 1), :] = value[r : r + 1, :]
+            place = (r % split_rows) * group + j % group
+            norm_rows[j // group, r // split_rows, pl.ds(place, 1), :] = value[r : r + 1, :]
 
     def step(i, carry):
         @pl.when(i < local_tokens)
@@ -378,6 +396,12 @@
         def _():
             finish(i - 4)
 
+        for k in range(groups_local):
+
+            @pl.when(i == 3 + group * (k + 1))
+            def _():
+                leave(k)
+
         return carry
 
     lax.fori_loop(0, local_tokens + 4, step, 0)
@@ -386,20 +410,6 @@
         gate_arrived(dp_at(q) * heads + h, 1 - u)
         gate_forward(q, 3).start()
 
-    split_rows = rows_local // toks
-    block = split_rows * local_tokens
-    for s in range(toks):
-        norm_send[s] = (
-            norm_rows[s * split_rows : (s + 1) * split_rows].reshape(block, dim).astype(BF16)
-        )
-
-    def norm_copy(q):
-        target = tok_at(q)
-        return remote(norm_send.at[target], norm_buf.at[t], nm_send.at[q], nm_recv.at[t], {"tok": target})
-
-    for q in range(1, toks):
-        norm_copy(q).start()
-    norm_buf[t] = norm_send[t]
     beside = gate_v.at[p * heads + (1 - h)]
     arrived(beside, gate_send.at[0, 0], gate_recv.at[p * heads + (1 - h), 0], sibling)
     for q in range(1, dps):
@@ -407,25 +417,33 @@
             gate_arrived(dp_at(q) * heads + (1 - h), half)
     for q in range(1, toks):
         source = tok_at(q)
-        arrived(norm_buf.at[source], nm_send.at[q], nm_recv.at[source], {"tok": source})
+        for k in range(groups_local):
+            arrived(norm_buf.at[source, k], nm_send.at[q, k], nm_recv.at[source, k], {"tok": source})
 
     gate_row = gbias[...].reshape(1, dim)
-    states = norm_buf[...].reshape(toks * block, dim)
+    block = group * split_rows
+    count = toks * groups_local
+    states = norm_buf[...].reshape(count * block, dim)
     columns = gate_v.shape[3]
     for c in range(dps * heads):
         cut = slice(c * columns, (c + 1) * columns)
         logits = jnp.dot(states, gate_v[c].reshape(dim, columns), preferred_element_type=F32) + gate_row[:, cut]
-        kept = norm_buf[:, :, cut].reshape(toks * block, columns).astype(F32)
-        gated = (kept * jax.nn.sigmoid(logits)).reshape(toks, split_rows, local_tokens, columns)
+        kept = norm_buf[:, :, :, cut].reshape(count * block, columns).astype(F32)
+        gated = kept * jax.nn.sigmoid(logits)
+        for b in range(count):
+            for r in range(split_rows):
+                first_row = b * block + r * group
+                result[r, b * group : (b + 1) * group, :] = gated[first_row : first_row + group, :]
         for r in range(split_rows):
-            out[0, r, :, cut] = gated[:, r].reshape(total_tokens, columns).astype(BF16)
+            out[0, r, :, cut] = result[r].astype(BF16)
 
     for q in range(1, toks):
         low_copy(q).wait_send()
         route_copy(q).wait_send()
         for c in range(chunks):
             head_copy(q, c).wait_send()
-        norm_copy(q).wait_send()
+        for k in range(groups_local):
+            norm_copy(q, k).wait_send()
     for q in range(dps):
         gate_copy(q).wait_send()
     for q in range(1, dps):
@@ -455,7 +473,7 @@
     hidden = expand_weight.shape[2]
     wide = dim // toks
     split_rows = rows // toks
-    block = split_rows * local
+    halves = split_rows * local // 16
     vmem = pl.BlockSpec(memory_space=pltpu.VMEM)
     anywhere = pl.BlockSpec(memory_space=pl.ANY)
     dma = pltpu.SemaphoreType.DMA
@@ -477,16 +495,17 @@
         pltpu.VMEM((local, dps, rows, dim), BF16),
         pltpu.VMEM((local, dps - 1, rows, dim), BF16),
         pltpu.VMEM((local, dps - 1, rows, dim), BF16),
-        pltpu.VMEM((rows, local, dim), F32),
-        pltpu.VMEM((toks, block, dim), BF16),
-        pltpu.VMEM((toks, block, dim), BF16),
+        pltpu.VMEM((halves, toks, 16, dim), F32),
+        pltpu.VMEM((toks, halves, 16, dim), BF16),
+        pltpu.VMEM((toks, halves, 16, dim), BF16),
         pltpu.VMEM((feats, feats), BF16),
+        pltpu.VMEM((split_rows, toks * local, gate_weight.shape[1]), F32),
         dma((3, local)), dma, dma((4, dps)), dma((slots, 2)),
         dma((toks,)), dma((toks,)), dma((toks,)), dma((toks,)),
         dma((toks, local // 2)), dma((toks, local // 2)),
         dma((local, dps)), dma((local, slots)), dma((local, dps)),
         dma((local,)), dma((local,)), dma((local, dps)), dma((local, dps)),
-        dma((toks,)), dma((toks,)),
+        dma((toks, halves)), dma((toks, halves)),
     ]
     gate_halves = gate_weight.reshape(2, -1, gate_weight.shape[1])
     return pl.pallas_call(
@@ -521,6 +540,7 @@
         and (features.shape[1] // toks) % 128 == 0
         and features.shape[0] // toks * local % 16 == 0
         and local % 8 == 0
+        and 16 % (features.shape[0] // toks) == 0
     )
     return (fused_device if fits else plain_device)(*arrays)
 

time: 57.2 us -> 53.8 us (0.941)
  Pallas kernels: 55.2 us -> 51.9 us
    pallas_call x1, Pallas kernels: 55.2 us -> 51.9 us  [fused_device(): pl.pallas_call(functools.partial(fused_kernel, toks, dps, heads), out_sha...]
where the time goes in v4:
time: 53.8 us; the launch traced here: 53.6 us
  Pallas kernels  51.9 us (96%)
  local copies, waits for them, and re-layouts  1.77 us (3%)
    pallas_call x1, Pallas kernels, fused_device(): pl.pallas_call(functools.partial(fused_kernel, toks, dps, heads), out_sha...  51.9 us
    unnamed x1, local copies, waits for them, and re-layouts  1.77 us

profile of v4, /device:TPU:0, one launch (start us, length us, event | category | flops | bytes accessed | tf_op | source)
XLA Modules:
  0.0 53.6 jit_solution(17337625709987426110)
XLA Ops:
  0.0 51.9 %shard_map.145 = bf16[1,4,32,1536]{3,2,1,0:T(8,128)(2,1)} custom-call(bf16[16,1024]{1,0:T(8,128)(2,1)} %feat.1, bf16[1024,512]{1,0:T(8,128)(2,1)} %cdown.1, bf16[512,1024]{1,0:T(8,128)(2,1)} %cup.1, f32[1,1024]{1,0:T(1,128)} %bitcast.4, s32[8,128]{1,0:T(8,128)} %bitcast.5, f32[8,1536]{1,0:T(8,128)} %pbias.1, f32[8,1536]{1,0:T(8,128)} %mgain.1, ...), custom_call_target="tpu_custom_call" | custom-call | tf_op jit(solution)/shard_map/pallas_call | solution.py:511
  51.9 1.8 %copy.17 = bf16[1,4,32,1536]{3,2,1,0:T(8,128)(2,1)} copy(bf16[1,4,32,1536]{3,2,1,0:T(8,128)(2,1)} %shard_map.145) | data formatting | bytes 786432
